TPU v7x, 32 devices: a whole 2x2x4 slice. The times are simulated.
32 devices in a mesh: groups: 2 (over y), band: 4 (over z), lev: 2 (over x), rd: 2 (over core).
Axes of the slice: x: 2, y: 2, z: 4, core: 2. Of those that a mesh axis runs over, the one named last changes fastest.
Arguments:
- departures: bfloat16 [2048, 8, 128], P(('groups', 'band', 'rd'), 'lev'), parts along dimension 0, may hold values from -6 to 6
- destinations: int32 [2048, 1], P(('groups', 'band', 'rd')), parts along dimension 0, may hold values from 0 to 3; in each aligned block of 128 rows (0 to 127, 128 to 255, ...) at most 64 rows name the same one
- tile_index: int32 [2048], P(('groups', 'band', 'rd')), parts along dimension 0, may hold values from 0 to 895
- obs_count: int32 [2048], P(('groups', 'band', 'rd')), parts along dimension 0, may hold values from 1 to 128
- interp_weights: bfloat16 [2048, 128, 128], P(('groups', 'band', 'rd')), parts along dimension 0, may hold values from -0.5 to 0.5
- background: float32 [16, 64, 7168], P(('groups', 'lev', 'rd'), 'band'), parts along dimension 0, may hold values from -6 to 6
- lon_taps: float32 [17, 7168], replicated, may hold values from 0.1 to 0.5
- lat_taps: float32 [17, 64], replicated, may hold values from 0.1 to 0.5
Outputs:
- filtered: float32 [16, 64, 7168], P(('groups', 'lev', 'rd'), 'band'), parts along dimension 0
There are 2 independent parts, one for each index of `groups`. A program takes and returns all parts, laid end to end along the dimension named above; an argument that names none is the same for every part. Nothing has to cross between parts.
Inputs may be any that keep to these rules, and one draw needn't show every extreme that they name: `destinations`: among the 128 blocks of one reader device, no band is named by more than 64 blocks.
All inputs are finite; a program needn't handle non-finite values.
Results may differ from a plain program's by a relative error of at most 0.0003.
Values sent between devices are 32-bit elements; how exact they have to be, the bound alone decides.
A program may use at most 64 MiB of HBM per device.

v0:
```python
import jax
import jax.numpy as jnp
from jax import lax
from jax.sharding import PartitionSpec as P

NLON = 7168
OBS = 128
TILE = 128
REACH = 8
SLAB_DEV = 2
LAT_DEV = 16
BLK_DEV = 128
TILES = 896


def padded_2(block, sides, width):
    for axis, dim in sides:
        count = lax.axis_size(axis)
        forward = [(i, i + 1) for i in range(count - 1)]
        backward = [(target, source) for source, target in forward]
        low = lax.ppermute(
            lax.slice_in_dim(block, block.shape[dim] - width, None, axis=dim), axis, forward
        )
        high = lax.ppermute(lax.slice_in_dim(block, 0, width, axis=dim), axis, backward)
        block = jnp.concatenate([low, block, high], axis=dim)
    return block


def lon_filter(gridded, coefficients):
    width = gridded.shape[2]
    padded = jnp.concatenate(
        [gridded[:, :, width - REACH :], gridded, gridded[:, :, :REACH]], axis=2
    )
    result = jnp.zeros(gridded.shape, jnp.float32)
    for offset in range(2 * REACH + 1):
        result = (
            result + coefficients[offset][None, None, :] * padded[:, :, offset : offset + width]
        )
    return result


def lat_filter(padded, coefficients, row_count):
    result = jnp.zeros((padded.shape[0], row_count, padded.shape[2]), jnp.float32)
    for offset in range(2 * REACH + 1):
        result = (
            result + coefficients[offset][None, :, None] * padded[:, offset : offset + row_count, :]
        )
    return result


def on_device(
    departures, destinations, tile_index, obs_count, interp_weights, background, lon_taps, lat_taps
):
    band_count = lax.axis_size("band")
    readers = lax.axis_size("rd")
    capacity = max(2, 2 * BLK_DEV // band_count)
    blocks = departures.shape[0]
    targets = destinations[:, 0]
    positions = jnp.arange(OBS, dtype=jnp.int32)
    retained = (positions[None, :] < obs_count[:, None]).astype(jnp.bfloat16)
    masked = departures * retained[:, None, :]
    values = jnp.einsum("bso,boc->bsc", masked, interp_weights, preferred_element_type=jnp.float32)
    values = values.reshape(blocks, readers, SLAB_DEV, TILE)
    chosen = (targets[:, None] == jnp.arange(band_count, dtype=jnp.int32)[None, :]).astype(
        jnp.int32
    )
    earlier = jnp.cumsum(chosen, axis=0) - chosen
    slot_rank = jnp.sum(earlier * chosen, axis=1)
    outbox = (
        jnp.zeros((band_count, readers, capacity, SLAB_DEV, TILE), jnp.float32)
        .at[targets, :, slot_rank]
        .set(values)
    )
    spread_tiles = jnp.broadcast_to(tile_index[:, None], (blocks, readers))
    labels = (
        jnp.zeros((band_count, readers, capacity), jnp.int32)
        .at[targets, :, slot_rank]
        .set(spread_tiles)
    )
    received, tiles_in = (
        lax.all_to_all(
            outbox.reshape(band_count * readers, capacity, SLAB_DEV, TILE),
            ("band", "rd"),
            split_axis=0,
            concat_axis=0,
            tiled=True,
        ),
        lax.all_to_all(
            labels.reshape(band_count * readers, capacity),
            ("band", "rd"),
            split_axis=0,
            concat_axis=0,
            tiled=True,
        ),
    )
    slot_count = band_count * readers * capacity
    received = received.reshape(slot_count, SLAB_DEV, TILE)
    tiles_in = tiles_in.reshape(slot_count)
    increment = (
        jnp.zeros((SLAB_DEV, TILES, TILE), jnp.float32)
        .at[:, tiles_in, :]
        .add(jnp.moveaxis(received, 1, 0))
    )
    summed = background + increment.reshape(SLAB_DEV, LAT_DEV, NLON)
    along_lon = lon_filter(summed, lon_taps)
    padded = padded_2(along_lon, (("band", 1),), REACH)
    first_row = lax.axis_index("band") * LAT_DEV
    row_weights = lax.dynamic_slice_in_dim(lat_taps, first_row, LAT_DEV, 1)
    return lat_filter(padded, row_weights, LAT_DEV)


def solution(mesh):
    return jax.shard_map(
        on_device,
        mesh=mesh,
        in_specs=(
            P(("groups", "band", "rd"), "lev", None),
            P(("groups", "band", "rd"), None),
            P(("groups", "band", "rd")),
            P(("groups", "band", "rd")),
            P(("groups", "band", "rd"), None, None),
            P(("groups", "lev", "rd"), "band", None),
            P(),
            P(),
        ),
        out_specs=P(("groups", "lev", "rd"), "band", None),
        check_vma=False,
    )
```

profile of v0, /device:TPU:0, one launch (start us, length us, event | category | flops | bytes accessed | tf_op | source)
XLA Modules:
  0.0 99.8 jit_solution(9616346158645906504)
XLA Ops:
  0.0 0.7 fusion.95
  0.7 0.2 reduce_window_sum.11
  0.9 0.8 select_reduce_fusion
  1.7 0.7 fusion.98
  2.4 0.7 broadcast_in_dim.10
  3.2 0.0 copy-start.1
  3.2 6.9 %scatter_fusion = s32[4,2,64]{1,2,0:T(8,128)S(1)} fusion(s32[4,2,64]{1,2,0:T(8,128)S(1)} %broadcast_in_dim.9, s32[128]{0:T(128)S(1)} %fusion.98, s32[128,2]{1,0:T(8,128)S(1)} %broadcast_in_dim.10), kind=kCustom, calls=%fused_computation | custom fusion | bytes 4096 | tf_op jit(solution)/shard_map/scatter | solution.py:78
  10.1 0.7 copy.11
  10.8 6.3 %all-to-all-start = ((s32[8,1,64]{2,1,0:T(1,128)}), s32[8,1,64]{2,1,0:T(1,128)S(1)}, u32[]{:S(2)}, u32[]{:S(2)}) async-start(s32[8,1,64]{2,1,0:T(1,128)} %bitcast.6), calls=%async_computation | async-start | bytes 8192 | tf_op jit(solution)/shard_map/all_to_all | solution.py:88
  17.1 0.7 fusion.96
  17.9 3.5 %fusion.92 = f32[128,4,128]{2,1,0:T(4,128)S(1)} fusion(bf16[128,128,128]{2,1,0:T(8,128)(2,1)} %param.12, bf16[128,4,128]{2,1,0:T(4,128)(2,1)} %param.8, bf16[128,128]{1,0:T(8,128)(2,1)S(1)} %fusion.96), kind=kOutput, calls=%fused_computation.151 | convolution fusion | flops 17039360 | bytes 4620288 | tf_op jit(solution)/shard_map/bso,boc->bsc/dot_general | solution.py:62
  21.3 1.0 broadcast_in_dim.11
  22.3 13.4 %scatter_fusion.1 = f32[4,2,64,2,128]{4,3,2,1,0:T(2,128)} fusion(f32[4,2,64,2,128]{4,3,2,1,0:T(2,128)} %broadcast_in_dim.11, s32[128]{0:T(128)S(1)} %fusion.98, f32[128,2,2,128]{3,2,1,0:T(2,128)S(1)} %bitcast.67), kind=kCustom, calls=%fused_computation.1 | custom fusion | bytes 787456 | tf_op jit(solution)/shard_map/scatter | solution.py:72
  35.8 0.0 all-to-all-done
  35.8 5.2 %all-to-all-start.1 = ((f32[8,64,2,128]{3,2,1,0:T(2,128)}), f32[8,64,2,128]{3,2,1,0:T(2,128)S(1)}, u32[]{:S(2)}, u32[]{:S(2)}) async-start(f32[8,64,2,128]{3,2,1,0:T(2,128)} %bitcast.9), calls=%async_computation.1 | async-start | bytes 1048576 | tf_op jit(solution)/shard_map/all_to_all | solution.py:81
  41.0 1.0 %fusion.101 = (f32[1,7168]{1,0:T(1,128)S(1)}, f32[1,7168]{1,0:T(1,128)S(1)}, f32[1,7168]{1,0:T(1,128)S(1)}, f32[1,7168]{1,0:T(1,128)S(1)}, f32[1,7168]{1,0:T(1,1...) fusion(f32[17,7168]{1,0:T(8,128)S(1)} %copy-done.1), kind=kLoop, calls=%fused_computation.186 | loop fusion | bytes 974848 | tf_op jit(solution)/shard_map/slice | solution.py:37
  42.0 0.6 broadcast.99
  42.6 0.7 reduce.3
  43.3 0.1 reshape.114
  43.4 13.0 %all-to-all-done.1 = f32[8,64,2,128]{3,2,1,0:T(2,128)S(1)} async-done(((f32[8,64,2,128]{3,2,1,0:T(2,128)}), f32[8,64,2,128]{3,2,1,0:T(2,128)S(1)}, u32[]{:S(2)}, u32[]{:S(2)}) %all-to-all-start.1) | async-done | bytes 524320 | tf_op jit(solution)/shard_map/all_to_all | solution.py:81
  56.4 0.2 broadcast_in_dim.8
  56.6 0.0 copy-start.2
  56.6 0.0 copy-start.3
  56.6 0.0 copy-start.4
  56.6 0.0 copy-start.5
  56.6 0.0 copy-start.6
  56.6 0.0 copy-start.7
  56.7 0.0 copy-start.8
  56.7 0.0 copy-start.9
  56.7 0.0 copy-start.10
  56.7 0.0 copy-start.11
  56.7 0.0 copy-start.12
  56.7 0.0 copy-start.13
  56.7 0.0 copy-start.14
  56.7 17.8 %scatter_fusion.2 = f32[2,896,128]{2,0,1:T(2,128)S(1)} fusion(f32[2,896,128]{2,0,1:T(2,128)S(1)} %broadcast_in_dim.8, s32[512]{0:T(512)S(1)} %bitcast.85, f32[512,2,128]{2,1,0:T(2,128)S(1)} %bitcast.66), kind=kCustom, calls=%fused_computation.2 | custom fusion | flops 131072 | bytes 1574912 | tf_op jit(solution)/shard_map/scatter-add | solution.py:102
  74.5 0.1 copy.13
  74.6 0.0 copy-start.15
  74.6 0.1 reshape.118
  74.8 0.1 add.138
  74.9 0.1 fusion.100
  75.0 6.2 %fusion.47 = f32[2,16,7168]{2,1,0:T(8,128)S(1)} fusion(f32[2,16,8]{2,1,0:T(8,128)S(1)} %get-tuple-element.8, f32[2,16,8]{2,1,0:T(8,128)S(1)} %get-tuple-element.7, f32[2,16,7168]{2,1,0:T(8,128)S(1)} %add.138, f32[7168]{0:T(1024)S(1)} %bitcast.83, f32[7168]{0:T(1024)S(1)} %bitcast.84, f32[7168]{0:T(1024)S(1)} %bitcast.69, f32[7168]{0:T(1024)S(1)} %bitcast.70, ...), kind=kLoop, calls=%fused_computation.92 | loop fusion | flops 11239424 | bytes 2324480 | tf_op jit(solution)/shard_map/add | solution.py:37
  81.3 0.1 fusion.99
  81.3 1.3 %collective-permute-start.1 = (f32[2,8,7168]{2,1,0:T(8,128)S(1)}, f32[2,8,7168]{2,1,0:T(8,128)S(1)}, u32[]{:S(2)}, u32[]{:S(2)}) collective-permute-start(f32[2,8,7168]{2,1,0:T(8,128)S(1)} %get-tuple-element.6), channel_id=1, source_target_pairs={{4,0},{8,4},{12,8},{5,1},{9,5},{13,9},{6,2},{10,6},{14,10},{7,3},{... | collective-permute-start | bytes 1376264 | tf_op jit(solution)/shard_map/ppermute | solution.py:24
  82.6 4.6 %collective-permute-start = (f32[2,8,7168]{2,1,0:T(8,128)S(1)}, f32[2,8,7168]{2,1,0:T(8,128)S(1)}, u32[]{:S(2)}, u32[]{:S(2)}) collective-permute-start(f32[2,8,7168]{2,1,0:T(8,128)S(1)} %get-tuple-element.5), channel_id=1, source_target_pairs={{0,4},{4,8},{8,12},{1,5},{5,9},{9,13},{2,6},{6,10},{10,14},{3,7},{... | collective-permute-start | bytes 1376264 | tf_op jit(solution)/shard_map/ppermute | solution.py:21
  87.2 0.1 dynamic-slice_bitcast_fusion.16
  87.4 7.9 %collective-permute-done.1 = f32[2,8,7168]{2,1,0:T(8,128)S(1)} collective-permute-done((f32[2,8,7168]{2,1,0:T(8,128)S(1)}, f32[2,8,7168]{2,1,0:T(8,128)S(1)}, u32[]{:S(2)}, u32[]{:S(2)}) %collective-permute-start.1) | collective-permute-done | bytes 458784 | tf_op jit(solution)/shard_map/ppermute | solution.py:24
  95.3 1.2 %collective-permute-done = f32[2,8,7168]{2,1,0:T(8,128)S(1)} collective-permute-done((f32[2,8,7168]{2,1,0:T(8,128)S(1)}, f32[2,8,7168]{2,1,0:T(8,128)S(1)}, u32[]{:S(2)}, u32[]{:S(2)}) %collective-permute-start) | collective-permute-done | bytes 458784 | tf_op jit(solution)/shard_map/ppermute | solution.py:21
  96.5 3.3 %fusion.3 = f32[2,16,7168]{2,1,0:T(8,128)} fusion(f32[2,16,7168]{2,1,0:T(8,128)S(1)} %fusion.47, f32[2,8,7168]{2,1,0:T(8,128)S(1)} %collective-permute-done.1, f32[2,8,7168]{2,1,0:T(8,128)S(1)} %collective-permute-done, f32[16]{0:T(128)S(1)} %get-tuple-element.42, f32[16]{0:T(128)S(1)} %get-tuple-element.27, f32[16]{0:T(128)S(1)} %get-tuple-element.28, ...), kind=kLoop, calls=%fused_computation.48 | loop fusion | flops 11239424 | bytes 2753600 | tf_op jit(solution)/shard_map/add | solution.py:46
  (19 shorter events, 0.1 us)
Async XLA Ops:
  3.2 37.8 %copy-start.1 = (f32[17,7168]{1,0:T(8,128)S(1)}, f32[17,7168]{1,0:T(8,128)}, u32[]{:S(2)}) copy-start(f32[17,7168]{1,0:T(8,128)} %param.14) | copy-start | bytes 1462276
  10.8 25.0 %all-to-all-start = ((s32[8,1,64]{2,1,0:T(1,128)}), s32[8,1,64]{2,1,0:T(1,128)S(1)}, u32[]{:S(2)}, u32[]{:S(2)}) async-start(s32[8,1,64]{2,1,0:T(1,128)} %bitcast.6), calls=%async_computation | async-start | bytes 8192 | tf_op jit(solution)/shard_map/all_to_all | solution.py:88
  35.8 39.0 %copy-start = (f32[2,16,7168]{2,1,0:T(8,128)S(1)}, f32[2,16,7168]{2,1,0:T(8,128)}, u32[]{:S(2)}) copy-start(f32[2,16,7168]{2,1,0:T(8,128)} %param.13) | copy-start | bytes 2752516
  35.8 20.6 %all-to-all-start.1 = ((f32[8,64,2,128]{3,2,1,0:T(2,128)}), f32[8,64,2,128]{3,2,1,0:T(2,128)S(1)}, u32[]{:S(2)}, u32[]{:S(2)}) async-start(f32[8,64,2,128]{3,2,1,0:T(2,128)} %bitcast.9), calls=%async_computation.1 | async-start | bytes 1048576 | tf_op jit(solution)/shard_map/all_to_all | solution.py:81
  56.6 18.3 %copy-start.2 = (f32[1,7168]{1,0:T(1,128)S(1)}, f32[1,7168]{1,0:T(1,128)}, u32[]{:S(2)}) copy-start(f32[1,7168]{1,0:T(1,128)} %get-tuple-element.13) | copy-start | bytes 86020
  56.6 18.3 %copy-start.3 = (f32[1,7168]{1,0:T(1,128)S(1)}, f32[1,7168]{1,0:T(1,128)}, u32[]{:S(2)}) copy-start(f32[1,7168]{1,0:T(1,128)} %get-tuple-element.14) | copy-start | bytes 86020
  56.6 18.3 %copy-start.4 = (f32[1,7168]{1,0:T(1,128)S(1)}, f32[1,7168]{1,0:T(1,128)}, u32[]{:S(2)}) copy-start(f32[1,7168]{1,0:T(1,128)} %get-tuple-element.15) | copy-start | bytes 86020
  56.6 18.3 %copy-start.5 = (f32[1,7168]{1,0:T(1,128)S(1)}, f32[1,7168]{1,0:T(1,128)}, u32[]{:S(2)}) copy-start(f32[1,7168]{1,0:T(1,128)} %get-tuple-element.16) | copy-start | bytes 86020
  56.6 18.3 %copy-start.6 = (f32[1,7168]{1,0:T(1,128)S(1)}, f32[1,7168]{1,0:T(1,128)}, u32[]{:S(2)}) copy-start(f32[1,7168]{1,0:T(1,128)} %get-tuple-element.17) | copy-start | bytes 86020
  56.6 18.3 %copy-start.7 = (f32[1,7168]{1,0:T(1,128)S(1)}, f32[1,7168]{1,0:T(1,128)}, u32[]{:S(2)}) copy-start(f32[1,7168]{1,0:T(1,128)} %get-tuple-element.18) | copy-start | bytes 86020
  56.7 18.3 %copy-start.8 = (f32[1,7168]{1,0:T(1,128)S(1)}, f32[1,7168]{1,0:T(1,128)}, u32[]{:S(2)}) copy-start(f32[1,7168]{1,0:T(1,128)} %get-tuple-element.19) | copy-start | bytes 86020
  56.7 18.3 %copy-start.9 = (f32[1,7168]{1,0:T(1,128)S(1)}, f32[1,7168]{1,0:T(1,128)}, u32[]{:S(2)}) copy-start(f32[1,7168]{1,0:T(1,128)} %get-tuple-element.20) | copy-start | bytes 86020
  56.7 18.3 %copy-start.10 = (f32[1,7168]{1,0:T(1,128)S(1)}, f32[1,7168]{1,0:T(1,128)}, u32[]{:S(2)}) copy-start(f32[1,7168]{1,0:T(1,128)} %get-tuple-element.21) | copy-start | bytes 86020
  56.7 18.3 %copy-start.11 = (f32[1,7168]{1,0:T(1,128)S(1)}, f32[1,7168]{1,0:T(1,128)}, u32[]{:S(2)}) copy-start(f32[1,7168]{1,0:T(1,128)} %get-tuple-element.22) | copy-start | bytes 86020
  56.7 18.3 %copy-start.12 = (f32[1,7168]{1,0:T(1,128)S(1)}, f32[1,7168]{1,0:T(1,128)}, u32[]{:S(2)}) copy-start(f32[1,7168]{1,0:T(1,128)} %get-tuple-element.23) | copy-start | bytes 86020
  56.7 18.3 %copy-start.13 = (f32[1,7168]{1,0:T(1,128)S(1)}, f32[1,7168]{1,0:T(1,128)}, u32[]{:S(2)}) copy-start(f32[1,7168]{1,0:T(1,128)} %get-tuple-element.24) | copy-start | bytes 86020
  56.7 18.3 %copy-start.14 = (f32[1,7168]{1,0:T(1,128)S(1)}, f32[1,7168]{1,0:T(1,128)}, u32[]{:S(2)}) copy-start(f32[1,7168]{1,0:T(1,128)} %get-tuple-element.25) | copy-start | bytes 86020
  74.6 12.6 %copy-start.15 = (f32[17,64]{1,0:T(8,128)S(1)}, f32[17,64]{1,0:T(8,128)}, u32[]{:S(2)}) copy-start(f32[17,64]{1,0:T(8,128)} %param.15) | copy-start | bytes 13060
  81.3 14.0 %collective-permute-start.1 = (f32[2,8,7168]{2,1,0:T(8,128)S(1)}, f32[2,8,7168]{2,1,0:T(8,128)S(1)}, u32[]{:S(2)}, u32[]{:S(2)}) collective-permute-start(f32[2,8,7168]{2,1,0:T(8,128)S(1)} %get-tuple-element.6), channel_id=1, source_target_pairs={{4,0},{8,4},{12,8},{5,1},{9,5},{13,9},{6,2},{10,6},{14,10},{7,3},{... | collective-permute-start | bytes 1376264 | tf_op jit(solution)/shard_map/ppermute | solution.py:24
  82.6 13.8 %collective-permute-start = (f32[2,8,7168]{2,1,0:T(8,128)S(1)}, f32[2,8,7168]{2,1,0:T(8,128)S(1)}, u32[]{:S(2)}, u32[]{:S(2)}) collective-permute-start(f32[2,8,7168]{2,1,0:T(8,128)S(1)} %get-tuple-element.5), channel_id=1, source_target_pairs={{0,4},{4,8},{8,12},{1,5},{5,9},{9,13},{2,6},{6,10},{10,14},{3,7},{... | collective-permute-start | bytes 1376264 | tf_op jit(solution)/shard_map/ppermute | solution.py:21
where the time goes:
time: 100 us; the launch traced here: 99.8 us
  other arithmetic  31.3 us (31%)
  local copies, waits for them, and re-layouts  25.3 us (25%)
  waiting for transfers between devices  22.1 us (22%)
  starting transfers between devices  17.4 us (17%)
  matrix products  3.45 us (3%)
    scatter-add x1, other arithmetic, on_device(): increment = jnp.zeros((SLAB_DEV, TILES, TILE), jnp.float32).at[:, tiles_i...  17.8 us
    scatter x1, local copies, waits for them, and re-layouts, on_device(): outbox = jnp.zeros((band_count, readers, capacity, SLAB_DEV, TILE), jnp.f...  13.4 us
    all_to_all x1, waiting for transfers between devices, on_device(): lax.all_to_all(outbox.reshape(band_count * readers, capacity, SLAB_DEV, T...  13 us
    ppermute x1, waiting for transfers between devices, padded_2(): lax.ppermute(lax.slice_in_dim(block, 0, width, axis=dim), axis, backward)  7.91 us
    scatter x2, local copies, waits for them, and re-layouts, on_device(): labels = jnp.zeros((band_count, readers, capacity), jnp.int32).at[targets...  7.62 us
    all_to_all x1, starting transfers between devices, on_device(): lax.all_to_all(labels.reshape(band_count * readers, capacity), ('band', '...  6.33 us
    add x1, other arithmetic, lon_filter(): result + coefficients[offset][None, None, :] * padded[:, :, offset:offset...  6.22 us
    all_to_all x1, starting transfers between devices, on_device(): lax.all_to_all(outbox.reshape(band_count * readers, capacity, SLAB_DEV, T...  5.23 us
  transfers between devices with their start and end apart: 4, of which 3 were waited for; matrix products, arithmetic and copies ran while one was open for 21% of the time, Pallas kernels for 0%

commit v1 on v0

v1 whole, which is shorter than its diff:
```python
import functools

import jax
import jax.numpy as jnp
from jax import lax
from jax.experimental import pallas as pl
from jax.experimental.pallas import tpu as pltpu
from jax.sharding import PartitionSpec as P

NLON = 7168
OBS = 128
TILE = 128
REACH = 8
SLAB_DEV = 2
LAT_DEV = 16
BLK_DEV = 128
ROW_TILES = NLON // TILE
TILES = ROW_TILES * LAT_DEV
TAPS = 2 * REACH + 1
SPAN = LAT_DEV + 2 * REACH
W_PARTS = 4
CHUNK_TILES = 7
CHUNK = CHUNK_TILES * TILE
CHUNKS = NLON // CHUNK
F32 = jnp.float32
BF16 = jnp.bfloat16
MESH = pl.DeviceIdType.MESH


def iota(shape, axis):
    return lax.broadcasted_iota(jnp.int32, shape, axis)


def split(value):
    high = value.astype(BF16)
    return high, (value - high.astype(F32)).astype(BF16)


def kernel(
    n_band,
    n_rd,
    cap,
    dep_ref,
    dest_ref,
    tile_ref,
    count_ref,
    w_hbm,
    bg_hbm,
    lon_hbm,
    lat_ref,
    out_hbm,
    w_v,
    values,
    outbox,
    inbox,
    onehot,
    field,
    along,
    lon_v,
    out_v,
    w_sem,
    bg_sem,
    lon_sem,
    out_sem,
    box_send,
    box_recv,
    halo_send,
    halo_recv,
):
    n_src = n_band * n_rd
    slots = n_band * cap
    per_group = TILE // cap
    groups = n_src // per_group
    band = lax.axis_index("band")
    rd = lax.axis_index("rd")
    me = band * n_rd + rd

    w_copies = []
    part = BLK_DEV // W_PARTS
    for i in range(W_PARTS):
        rows = pl.ds(i * part, part)
        w_copies.append(pltpu.make_async_copy(w_hbm.at[rows], w_v.at[rows], w_sem.at[i]))
        w_copies[-1].start()
    bg_copies = []
    for s in range(SLAB_DEV):
        bg_copies.append(
            pltpu.make_async_copy(
                bg_hbm.at[s], field.at[s, :, pl.ds(TILE, NLON)], bg_sem.at[s]
            )
        )
        bg_copies[-1].start()
    lon_copy = pltpu.make_async_copy(lon_hbm, lon_v, lon_sem)
    lon_copy.start()

    barrier = pltpu.get_barrier_semaphore()

    def greet(step, carry):
        other = lax.rem(me + step, n_src)
        pl.semaphore_signal(
            barrier,
            inc=1,
            device_id={"band": other // n_rd, "rd": lax.rem(other, n_rd)},
            device_id_type=MESH,
        )
        return carry

    lax.fori_loop(1, n_src, greet, 0)

    square = (BLK_DEV, BLK_DEV)
    lane, sub = iota(square, 1), iota(square, 0)
    eye = lane == sub
    dest = jnp.broadcast_to(dest_ref[...], square)
    chosen = (dest == lane).astype(F32)
    before = (lane < sub).astype(BF16)
    earlier = jnp.dot(before, chosen.astype(BF16), preferred_element_type=F32)
    rank = jnp.sum(earlier * chosen, axis=1, keepdims=True)
    slot = dest_ref[...].astype(F32) * cap + rank
    slot_row = jnp.sum(jnp.where(eye, slot, 0.0), axis=0, keepdims=True)
    pack = (iota((slots, BLK_DEV), 0).astype(F32) == slot_row).astype(BF16)
    tile_row = tile_ref[...]
    lat_row = jnp.zeros_like(tile_row)
    for r in range(1, LAT_DEV):
        lat_row = lat_row + (tile_row >= r * ROW_TILES).astype(jnp.int32)
    place_row = (tile_row - lat_row * ROW_TILES) * LAT_DEV + lat_row + 1
    place = jnp.sum(jnp.where(eye, place_row.astype(F32), 0.0), axis=1, keepdims=True)
    shift = lax.rem(me, per_group) * cap
    lane_at = (lane - shift).astype(F32)
    label_of = jnp.where(lane_at == rank, place, 0.0)
    for d in range(n_band):
        row = jnp.sum(jnp.where(dest == d, label_of, 0.0), axis=0, keepdims=True)
        row = jnp.broadcast_to(row, (8, TILE))
        for r in range(n_rd):
            outbox[0, d * n_rd + r, pl.ds(cap, 8), :] = row

    lanes4 = iota((2 * SLAB_DEV, OBS), 1)
    for i in range(W_PARTS):
        w_copies[i].wait()

        def multiply(pair, carry, i=i):
            both = []
            for h in range(2):
                b = i * part + pair * 2 + h
                obs = jnp.where(lanes4 < count_ref[b], dep_ref[b].astype(F32), 0.0)
                both.append(jnp.dot(obs.astype(BF16), w_v[b], preferred_element_type=F32))
            at = pl.multiple_of((i * (part // 2) + pair) * 8, 8)
            values[pl.ds(at, 8), :] = jnp.concatenate(both, axis=0)
            return carry

        lax.fori_loop(0, part // 2, multiply, 0, unroll=8)

    pl.semaphore_wait(barrier, n_src - 1)

    def box_copy(s, step):
        other = lax.rem(me + step, n_src)
        size = cap + 8 if s == 0 else cap
        return pltpu.make_async_remote_copy(
            src_ref=outbox.at[s, other, pl.ds(0, size)],
            dst_ref=inbox.at[s, me, pl.ds(0, size)],
            send_sem=box_send.at[s, step],
            recv_sem=box_recv.at[s, step],
            device_id={"band": other // n_rd, "rd": lax.rem(other, n_rd)},
            device_id_type=MESH,
        )

    for s in range(SLAB_DEV):
        for r in range(n_rd):
            value = values[pl.ds(r * SLAB_DEV + s, BLK_DEV, stride=2 * SLAB_DEV), :]
            both = jnp.dot(
                pack, jnp.concatenate(split(value), axis=1), preferred_element_type=F32
            )
            both = both[:, :TILE] + both[:, TILE:]
            for d in range(n_band):
                outbox[s, d * n_rd + r, pl.ds(0, cap), :] = both[d * cap : (d + 1) * cap]

        def send(step, carry, s=s):
            box_copy(s, step).start()
            return carry

        lax.fori_loop(1, n_src, send, 0)
        inbox[s, me] = outbox[s, me]

    n_lat = lat_ref.shape[1]
    wide = (LAT_DEV, 128)
    own = iota((LAT_DEV, n_lat), 1) == iota((LAT_DEV, n_lat), 0) + band * LAT_DEV
    lane16, sub16 = iota(wide, 1), iota(wide, 0)
    third = lane16 // SPAN
    offset = lane16 - third * SPAN - sub16
    lat_matrix = jnp.zeros(wide, F32)
    for k in range(TAPS):
        column = jnp.sum(jnp.where(own, lat_ref[k : k + 1, :], 0.0), axis=1, keepdims=True)
        lat_matrix = lat_matrix + jnp.where(offset == k, column, 0.0)
    high = lat_matrix.astype(BF16).astype(F32)
    lat_matrix = jnp.where(third == 1, lat_matrix - high, high).astype(BF16)[:, : 3 * SPAN]

    @pl.when(band == 0)
    def _():
        along[:, pl.ds(0, REACH), :] = jnp.zeros((SLAB_DEV, REACH, NLON), F32)

    @pl.when(band == n_band - 1)
    def _():
        along[:, pl.ds(REACH + LAT_DEV, REACH), :] = jnp.zeros((SLAB_DEV, REACH, NLON), F32)

    def halo_copy(s, up):
        source = LAT_DEV if up else REACH
        target = 0 if up else REACH + LAT_DEV
        return pltpu.make_async_remote_copy(
            src_ref=along.at[s, pl.ds(source, REACH)],
            dst_ref=along.at[s, pl.ds(target, REACH)],
            send_sem=halo_send.at[s, int(up)],
            recv_sem=halo_recv.at[s, int(up)],
            device_id={"band": band + 1 if up else band - 1, "rd": rd},
            device_id_type=MESH,
        )

    for s in range(SLAB_DEV):

        def take(step, carry, s=s):
            box_copy(s, step).wait_recv()
            return carry

        bg_copies[s].wait()
        lax.fori_loop(1, n_src, take, 0)
        if s == 0:
            rows = iota((CHUNK_TILES * LAT_DEV, TILE), 0) + 1
            for g in range(groups):
                label = jnp.sum(
                    inbox[0, pl.ds(g * per_group, per_group), cap, :], axis=0, keepdims=True
                )

                def mark(c, carry, g=g, label=label):
                    at = pl.multiple_of(c * CHUNK_TILES * LAT_DEV, 16)
                    hit = (rows + at).astype(F32) == label
                    onehot[pl.ds(at, CHUNK_TILES * LAT_DEV), pl.ds(g * TILE, TILE)] = hit.astype(
                        F32
                    ).astype(BF16)
                    return carry

                lax.fori_loop(0, CHUNKS, mark, 0)
            lon_copy.wait()
        received = inbox[s, :, pl.ds(0, cap), :].reshape(n_src * cap, TILE)
        pieces = jnp.concatenate(split(received), axis=1)

        def add(c, carry, s=s, pieces=pieces):
            at = pl.multiple_of(c * CHUNK_TILES * LAT_DEV, 16)
            both = jnp.dot(
                onehot[pl.ds(at, CHUNK_TILES * LAT_DEV), :], pieces, preferred_element_type=F32
            )
            both = both[:, :TILE] + both[:, TILE:]
            for q in range(CHUNK_TILES):
                columns = pl.ds(pl.multiple_of((c * CHUNK_TILES + q + 1) * TILE, TILE), TILE)
                field[s, :, columns] += both[q * LAT_DEV : (q + 1) * LAT_DEV]
            return carry

        lax.fori_loop(0, CHUNKS, add, 0)
        field[s, :, pl.ds(0, TILE)] = field[s, :, pl.ds(NLON, TILE)]
        field[s, :, pl.ds(NLON + TILE, TILE)] = field[s, :, pl.ds(TILE, TILE)]

        def lon_filter(c, carry, s=s):
            at = pl.multiple_of(c * CHUNK, TILE)
            width = CHUNK + 2 * TILE
            window = field[s, :, pl.ds(at, width)]
            total = jnp.zeros((LAT_DEV, CHUNK), F32)
            for k in range(TAPS):
                moved = window if k == REACH else pltpu.roll(window, (REACH - k) % width, 1)
                total = total + lon_v[k : k + 1, pl.ds(at, CHUNK)] * moved[:, TILE : TILE + CHUNK]
            along[s, pl.ds(REACH, LAT_DEV), pl.ds(at, CHUNK)] = total
            return carry

        lax.fori_loop(0, CHUNKS, lon_filter, 0)

        @pl.when(band < n_band - 1)
        def _(s=s):
            halo_copy(s, True).start()

        @pl.when(band > 0)
        def _(s=s):
            halo_copy(s, False).start()

    out_copies = []
    for s in range(SLAB_DEV):

        @pl.when(band > 0)
        def _(s=s):
            halo_copy(s, True).wait_recv()

        @pl.when(band < n_band - 1)
        def _(s=s):
            halo_copy(s, False).wait_recv()

        def lat_filter(c, carry, s=s):
            columns = pl.ds(pl.multiple_of(c * CHUNK, TILE), CHUNK)
            high, low = split(along[s, :, columns])
            out_v[s, :, columns] = jnp.dot(
                lat_matrix,
                jnp.concatenate([high, high, low], axis=0),
                preferred_element_type=F32,
            )
            return carry

        lax.fori_loop(0, CHUNKS, lat_filter, 0)
        out_copies.append(pltpu.make_async_copy(out_v.at[s], out_hbm.at[s], out_sem.at[s]))
        out_copies[-1].start()

    for s in range(SLAB_DEV):

        def sent(step, carry, s=s):
            box_copy(s, step).wait_send()
            return carry

        lax.fori_loop(1, n_src, sent, 0)

        @pl.when(band < n_band - 1)
        def _(s=s):
            halo_copy(s, True).wait_send()

        @pl.when(band > 0)
        def _(s=s):
            halo_copy(s, False).wait_send()

        out_copies[s].wait()


def on_device(
    departures, destinations, tile_index, obs_count, interp_weights, background, lon_taps, lat_taps
):
    n_band = lax.axis_size("band")
    n_rd = lax.axis_size("rd")
    cap = max(2, 2 * BLK_DEV // n_band)
    n_src = n_band * n_rd
    vmem = pl.BlockSpec(memory_space=pltpu.VMEM)
    hbm = pl.BlockSpec(memory_space=pl.ANY)
    dma = pltpu.SemaphoreType.DMA
    return pl.pallas_call(
        functools.partial(kernel, n_band, n_rd, cap),
        out_shape=jax.ShapeDtypeStruct(background.shape, F32),
        in_specs=[
            vmem,
            vmem,
            vmem,
            pl.BlockSpec(memory_space=pltpu.SMEM),
            hbm,
            hbm,
            hbm,
            vmem,
        ],
        out_specs=hbm,
        scratch_shapes=[
            pltpu.VMEM((BLK_DEV, OBS, TILE), BF16),
            pltpu.VMEM((BLK_DEV * 2 * SLAB_DEV, TILE), F32),
            pltpu.VMEM((SLAB_DEV, n_src, cap + 8, TILE), F32),
            pltpu.VMEM((SLAB_DEV, n_src, cap + 8, TILE), F32),
            pltpu.VMEM((TILES, n_src * cap), BF16),
            pltpu.VMEM((SLAB_DEV, LAT_DEV, NLON + 2 * TILE), F32),
            pltpu.VMEM((SLAB_DEV, SPAN, NLON), F32),
            pltpu.VMEM((TAPS, NLON), F32),
            pltpu.VMEM((SLAB_DEV, LAT_DEV, NLON), F32),
            dma((W_PARTS,)),
            dma((SLAB_DEV,)),
            dma,
            dma((SLAB_DEV,)),
            dma((SLAB_DEV, n_src)),
            dma((SLAB_DEV, n_src)),
            dma((SLAB_DEV, 2)),
            dma((SLAB_DEV, 2)),
        ],
        compiler_params=pltpu.CompilerParams(
            collective_id=0, has_side_effects=True, vmem_limit_bytes=40 << 20
        ),
    )(
        departures,
        destinations,
        tile_index.reshape(1, BLK_DEV),
        obs_count,
        interp_weights,
        background,
        lon_taps,
        lat_taps,
    )


def solution(mesh):
    return jax.shard_map(
        on_device,
        mesh=mesh,
        in_specs=(
            P(("groups", "band", "rd"), "lev", None),
            P(("groups", "band", "rd"), None),
            P(("groups", "band", "rd")),
            P(("groups", "band", "rd")),
            P(("groups", "band", "rd"), None, None),
            P(("groups", "lev", "rd"), "band", None),
            P(),
            P(),
        ),
        out_specs=P(("groups", "lev", "rd"), "band", None),
        check_vma=False,
    )
```

time: 100 us -> 45.7 us (0.46)
  Pallas kernels: 0 us -> 36.3 us
  other arithmetic: 31.3 us -> 0 us
  waiting for transfers between devices: 22.1 us -> 0 us
  starting transfers between devices: 17.4 us -> 0 us
  local copies, waits for them, and re-layouts: 25.3 us -> 9.07 us
  matrix products: 3.45 us -> 0 us
    pallas_call x0 -> x1, Pallas kernels: none -> 36.3 us  [on_device(): pl.pallas_call(functools.partial(kernel, n_band, n_rd, cap), out_shape=ja...]
    scatter x3 -> x0, local copies, waits for them, and re-layouts: 21.1 us -> none  [the longest x1 13.4 us: on_device(): outbox = jnp.zeros((band_count, readers, capacity, SLAB_DEV, TILE), jnp.f...]
    scatter-add x1 -> x0, other arithmetic: 17.8 us -> none  [on_device(): increment = jnp.zeros((SLAB_DEV, TILES, TILE), jnp.float32).at[:, tiles_i...]
    all_to_all x2 -> x0, waiting for transfers between devices: 13 us -> none  [the longest x1 13 us: on_device(): lax.all_to_all(outbox.reshape(band_count * readers, capacity, SLAB_DEV, T...]
    all_to_all x2 -> x0, starting transfers between devices: 11.6 us -> none  [the longest x1 6.33 us: on_device(): lax.all_to_all(labels.reshape(band_count * readers, capacity), ('band', '...]
    add x3 -> x0, other arithmetic: 9.64 us -> none  [the longest x1 6.22 us: lon_filter(): result + coefficients[offset][None, None, :] * padded[:, :, offset:offset...]
    ppermute x2 -> x0, waiting for transfers between devices: 9.09 us -> none  [the longest x1 7.91 us: padded_2(): lax.ppermute(lax.slice_in_dim(block, 0, width, axis=dim), axis, backward)]
    unnamed x32 -> x16, local copies, waits for them, and re-layouts: 0.07 us -> 9.07 us
  transfers between devices with their start and end apart: 4 -> 0, of which waited for: 3 -> 0; matrix products, arithmetic and copies ran while one was open for 21% -> 0% of each run, Pallas kernels for 0% -> 0%
where the time goes in v1:
time: 45.7 us; the launch traced here: 45.4 us
  Pallas kernels  36.3 us (79%)
  local copies, waits for them, and re-layouts  9.07 us (20%)
    pallas_call x1, Pallas kernels, on_device(): pl.pallas_call(functools.partial(kernel, n_band, n_rd, cap), out_shape=ja...  36.3 us
    unnamed x16, local copies, waits for them, and re-layouts  9.07 us

profile of v1, /device:TPU:0, one launch (start us, length us, event | category | flops | bytes accessed | tf_op | source)
XLA Modules:
  0.0 45.4 jit_solution(8841261294775223297)
XLA Ops:
  0.0 0.8 %copy.9.dest_ref = s32[128,1]{1,0:T(8,128)S(1)} copy(s32[128,1]{0,1:T(1,128)} %param.9) | data formatting | bytes 1024 | tf_op args[1]
  0.8 0.0 copy-start
  0.8 2.2 %copy-done = bf16[128,128,128]{2,1,0:T(8,128)(2,1)S(1)} copy-done((bf16[128,128,128]{2,1,0:T(8,128)(2,1)S(1)}, bf16[128,128,128]{2,1,0:T(8,128)(2,1)}, u32[]{:S(2)}) %copy-start) | copy-done | bytes 4194328
  3.0 0.0 copy-start.1
  3.0 1.2 %copy-done.1 = f32[2,16,7168]{2,1,0:T(8,128)S(1)} copy-done((f32[2,16,7168]{2,1,0:T(8,128)S(1)}, f32[2,16,7168]{2,1,0:T(8,128)}, u32[]{:S(2)}) %copy-start.1) | copy-done | bytes 917528
  4.1 0.0 copy-start.2
  4.1 1.1 %copy-done.2 = f32[17,7168]{1,0:T(8,128)S(1)} copy-done((f32[17,7168]{1,0:T(8,128)S(1)}, f32[17,7168]{1,0:T(8,128)}, u32[]{:S(2)}) %copy-start.2) | copy-done | bytes 487448
  5.2 0.0 copy-start.3
  5.2 0.9 %copy-done.3 = bf16[128,4,128]{2,1,0:T(4,128)(2,1)S(1)} copy-done((bf16[128,4,128]{2,1,0:T(4,128)(2,1)S(1)}, bf16[128,4,128]{2,1,0:T(4,128)(2,1)}, u32[]{:S(2)}) %copy-start.3) | copy-done | bytes 131096
  6.1 0.0 copy-start.4
  6.1 0.7 %copy-done.4 = f32[17,64]{1,0:T(8,128)S(1)} copy-done((f32[17,64]{1,0:T(8,128)S(1)}, f32[17,64]{1,0:T(8,128)}, u32[]{:S(2)}) %copy-start.4) | copy-done | bytes 4376
  6.8 0.0 copy-start.5
  6.8 0.7 %copy-done.5 = s32[128]{0:T(128)S(1)} copy-done((s32[128]{0:T(128)S(1)}, s32[128]{0:T(128)}, u32[]{:S(2)}) %copy-start.5) | copy-done | bytes 536
  7.5 0.0 copy-start.6
  7.5 0.7 %copy-done.6 = s32[128]{0:T(128)S(1)} copy-done((s32[128]{0:T(128)S(1)}, s32[128]{0:T(128)}, u32[]{:S(2)}) %copy-start.6) | copy-done | bytes 536
  8.2 36.3 %shard_map.82 = f32[2,16,7168]{2,1,0:T(8,128)S(1)} custom-call(bf16[128,4,128]{2,1,0:T(4,128)(2,1)S(1)} %copy-done.3, s32[128,1]{1,0:T(8,128)S(1)} %copy.9.dest_ref, s32[1,128]{1,0:T(1,128)S(1)} %bitcast.1, s32[128]{0:T(128)S(1)} %copy-done.6, bf16[128,128,128]{2,1,0:T(8,128)(2,1)S(1)} %copy-done, f32[2,16,7168]{2,1,0:T(8,128)S(1)} %copy-done.1, ...), custom_call_target="tpu_custom_call" | custom-call | tf_op jit(solution)/shard_map/pallas_call | solution.py:333
  44.5 0.9 %copy.11 = f32[2,16,7168]{2,1,0:T(8,128)} copy(f32[2,16,7168]{2,1,0:T(8,128)S(1)} %shard_map.82) | data formatting | bytes 1835008
Async XLA Ops:
  0.8 2.2 %copy-start = (bf16[128,128,128]{2,1,0:T(8,128)(2,1)S(1)}, bf16[128,128,128]{2,1,0:T(8,128)(2,1)}, u32[]{:S(2)}) copy-start(bf16[128,128,128]{2,1,0:T(8,128)(2,1)} %w_hbm.1) | copy-start | bytes 12582916
  3.0 1.2 %copy-start.1 = (f32[2,16,7168]{2,1,0:T(8,128)S(1)}, f32[2,16,7168]{2,1,0:T(8,128)}, u32[]{:S(2)}) copy-start(f32[2,16,7168]{2,1,0:T(8,128)} %bg_hbm.1) | copy-start | bytes 2752516
  4.1 1.1 %copy-start.2 = (f32[17,7168]{1,0:T(8,128)S(1)}, f32[17,7168]{1,0:T(8,128)}, u32[]{:S(2)}) copy-start(f32[17,7168]{1,0:T(8,128)} %lon_hbm.1) | copy-start | bytes 1462276
  5.2 0.9 %copy-start.3 = (bf16[128,4,128]{2,1,0:T(4,128)(2,1)S(1)}, bf16[128,4,128]{2,1,0:T(4,128)(2,1)}, u32[]{:S(2)}) copy-start(bf16[128,4,128]{2,1,0:T(4,128)(2,1)} %dep_ref.1) | copy-start | bytes 393220
  6.1 0.7 %copy-start.4 = (f32[17,64]{1,0:T(8,128)S(1)}, f32[17,64]{1,0:T(8,128)}, u32[]{:S(2)}) copy-start(f32[17,64]{1,0:T(8,128)} %lat_ref.1) | copy-start | bytes 13060
  6.8 0.7 %copy-start.5 = (s32[128]{0:T(128)S(1)}, s32[128]{0:T(128)}, u32[]{:S(2)}) copy-start(s32[128]{0:T(128)} %param.10) | copy-start | bytes 1540
  7.5 0.7 %copy-start.6 = (s32[128]{0:T(128)S(1)}, s32[128]{0:T(128)}, u32[]{:S(2)}) copy-start(s32[128]{0:T(128)} %count_ref.1) | copy-start | bytes 1540

commit v2 on v1

--- a/solution.py
+++ b/solution.py
@@ -50,6 +50,7 @@
     lat_ref,
     out_hbm,
     w_v,
+    masked,
     values,
     outbox,
     inbox,
@@ -109,12 +110,18 @@
     square = (BLK_DEV, BLK_DEV)
     lane, sub = iota(square, 1), iota(square, 0)
     eye = lane == sub
-    dest = jnp.broadcast_to(dest_ref[...], square)
+
+
+    def column(row):
+        return jnp.sum(jnp.where(eye, row.astype(F32), 0.0), axis=1, keepdims=True)
+
+    dest_column = column(dest_ref[...])
+    dest = jnp.broadcast_to(dest_column, square).astype(jnp.int32)
     chosen = (dest == lane).astype(F32)
     before = (lane < sub).astype(BF16)
     earlier = jnp.dot(before, chosen.astype(BF16), preferred_element_type=F32)
     rank = jnp.sum(earlier * chosen, axis=1, keepdims=True)
-    slot = dest_ref[...].astype(F32) * cap + rank
+    slot = dest_column * cap + rank
     slot_row = jnp.sum(jnp.where(eye, slot, 0.0), axis=0, keepdims=True)
     pack = (iota((slots, BLK_DEV), 0).astype(F32) == slot_row).astype(BF16)
     tile_row = tile_ref[...]
@@ -122,7 +129,7 @@
     for r in range(1, LAT_DEV):
         lat_row = lat_row + (tile_row >= r * ROW_TILES).astype(jnp.int32)
     place_row = (tile_row - lat_row * ROW_TILES) * LAT_DEV + lat_row + 1
-    place = jnp.sum(jnp.where(eye, place_row.astype(F32), 0.0), axis=1, keepdims=True)
+    place = column(place_row)
     shift = lax.rem(me, per_group) * cap
     lane_at = (lane - shift).astype(F32)
     label_of = jnp.where(lane_at == rank, place, 0.0)
@@ -132,21 +139,37 @@
         for r in range(n_rd):
             outbox[0, d * n_rd + r, pl.ds(cap, 8), :] = row
 
-    lanes4 = iota((2 * SLAB_DEV, OBS), 1)
+    height = 2 * SLAB_DEV
+    rows_of = (BLK_DEV * height, BLK_DEV)
+    picked = jnp.where(
+        iota(rows_of, 0) // height == iota(rows_of, 1), count_ref[...].astype(F32), 0.0
+    )
+    counts = jnp.sum(picked, axis=1, keepdims=True)
+    wide_dep = dep_ref[...].astype(F32).reshape(rows_of)
+    masked[...] = jnp.where(iota(rows_of, 1).astype(F32) < counts, wide_dep, 0.0)
+    first = iota((4 * height, OBS), 0) % (2 * height) < height
     for i in range(W_PARTS):
         w_copies[i].wait()
 
-        def multiply(pair, carry, i=i):
-            both = []
-            for h in range(2):
-                b = i * part + pair * 2 + h
-                obs = jnp.where(lanes4 < count_ref[b], dep_ref[b].astype(F32), 0.0)
-                both.append(jnp.dot(obs.astype(BF16), w_v[b], preferred_element_type=F32))
-            at = pl.multiple_of((i * (part // 2) + pair) * 8, 8)
-            values[pl.ds(at, 8), :] = jnp.concatenate(both, axis=0)
-            return carry
-
-        lax.fori_loop(0, part // 2, multiply, 0, unroll=8)
+        def multiply(group, carry):
+            at = pl.multiple_of(group * 4 * height, 4 * height)
+            obs = masked[pl.ds(at, 4 * height), :]
+            left = jnp.concatenate(
+                [jnp.where(first, obs, 0.0), jnp.where(first, 0.0, obs)], axis=1
+            ).astype(BF16)
+            right = jnp.concatenate(
+                [
+                    w_v[pl.ds(group * 4, 2)].reshape(2 * OBS, TILE),
+                    w_v[pl.ds(group * 4 + 2, 2)].reshape(2 * OBS, TILE),
+                ],
+                axis=1,
+            )
+            product = jnp.dot(left, right, preferred_element_type=F32)
+            values[pl.ds(at, 2 * height), :] = product[: 2 * height, :TILE]
+            values[pl.ds(at + 2 * height, 2 * height), :] = product[2 * height :, TILE:]
+            return carry
+
+        lax.fori_loop(i * part // 4, (i + 1) * part // 4, multiply, 0, unroll=4)
 
     pl.semaphore_wait(barrier, n_src - 1)
 
@@ -187,8 +210,8 @@
     offset = lane16 - third * SPAN - sub16
     lat_matrix = jnp.zeros(wide, F32)
     for k in range(TAPS):
-        column = jnp.sum(jnp.where(own, lat_ref[k : k + 1, :], 0.0), axis=1, keepdims=True)
-        lat_matrix = lat_matrix + jnp.where(offset == k, column, 0.0)
+        tap = jnp.sum(jnp.where(own, lat_ref[k : k + 1, :], 0.0), axis=1, keepdims=True)
+        lat_matrix = lat_matrix + jnp.where(offset == k, tap, 0.0)
     high = lat_matrix.astype(BF16).astype(F32)
     lat_matrix = jnp.where(third == 1, lat_matrix - high, high).astype(BF16)[:, : 3 * SPAN]
 
@@ -328,7 +351,7 @@
     cap = max(2, 2 * BLK_DEV // n_band)
     n_src = n_band * n_rd
     vmem = pl.BlockSpec(memory_space=pltpu.VMEM)
-    hbm = pl.BlockSpec(memory_space=pl.ANY)
+    hbm = pl.BlockSpec(memory_space=pltpu.HBM)
     dma = pltpu.SemaphoreType.DMA
     return pl.pallas_call(
         functools.partial(kernel, n_band, n_rd, cap),
@@ -337,7 +360,7 @@
             vmem,
             vmem,
             vmem,
-            pl.BlockSpec(memory_space=pltpu.SMEM),
+            vmem,
             hbm,
             hbm,
             hbm,
@@ -346,6 +369,7 @@
         out_specs=hbm,
         scratch_shapes=[
             pltpu.VMEM((BLK_DEV, OBS, TILE), BF16),
+            pltpu.VMEM((BLK_DEV * 2 * SLAB_DEV, OBS), F32),
             pltpu.VMEM((BLK_DEV * 2 * SLAB_DEV, TILE), F32),
             pltpu.VMEM((SLAB_DEV, n_src, cap + 8, TILE), F32),
             pltpu.VMEM((SLAB_DEV, n_src, cap + 8, TILE), F32),
@@ -364,13 +388,13 @@
             dma((SLAB_DEV, 2)),
         ],
         compiler_params=pltpu.CompilerParams(
-            collective_id=0, has_side_effects=True, vmem_limit_bytes=40 << 20
+            collective_id=0, has_side_effects=True, vmem_limit_bytes=56 << 20
         ),
     )(
         departures,
-        destinations,
+        destinations.reshape(1, BLK_DEV),
         tile_index.reshape(1, BLK_DEV),
-        obs_count,
+        obs_count.reshape(1, BLK_DEV),
         interp_weights,
         background,
         lon_taps,

time: 45.7 us -> 38.7 us (0.85)
  local copies, waits for them, and re-layouts: 9.07 us -> 2.16 us
    unnamed x16 -> x1, local copies, waits for them, and re-layouts: 9.07 us -> 2.16 us
where the time goes in v2:
time: 38.7 us; the launch traced here: 38.5 us
  Pallas kernels  36.4 us (94%)
  local copies, waits for them, and re-layouts  2.16 us (6%)
    pallas_call x1, Pallas kernels, on_device(): pl.pallas_call(functools.partial(kernel, n_band, n_rd, cap), out_shape=ja...  36.4 us
    unnamed x1, local copies, waits for them, and re-layouts  2.16 us

profile of v2, /device:TPU:0, one launch (start us, length us, event | category | flops | bytes accessed | tf_op | source)
XLA Modules:
  0.0 38.5 jit_solution(1521946990814269636)
XLA Ops:
  0.0 36.4 %shard_map.82 = f32[2,16,7168]{2,1,0:T(8,128)} custom-call(bf16[128,4,128]{2,1,0:T(4,128)(2,1)} %dep_ref.1, s32[1,128]{1,0:T(1,128)} %bitcast.3, s32[1,128]{1,0:T(1,128)} %bitcast.4, s32[1,128]{1,0:T(1,128)} %bitcast.5, bf16[128,128,128]{2,1,0:T(8,128)(2,1)} %w_hbm.1, f32[2,16,7168]{2,1,0:T(8,128)} %bg_hbm.1, f32[17,7168]{1,0:T(8,128)} %lon_hbm.1, ...), custom_call_target="tpu_custom_call" | custom-call | tf_op jit(solution)/shard_map/pallas_call | solution.py:356
  36.4 2.2 %copy.10 = f32[2,16,7168]{2,1,0:T(8,128)} copy(f32[2,16,7168]{2,1,0:T(8,128)} %shard_map.82) | data formatting | bytes 1835008

commit v3 on v2

--- a/solution.py
+++ b/solution.py
@@ -22,6 +22,9 @@
 CHUNK_TILES = 7
 CHUNK = CHUNK_TILES * TILE
 CHUNKS = NLON // CHUNK
+PIECES = 4
+PIECE_CHUNKS = CHUNKS // PIECES
+PIECE = CHUNK * PIECE_CHUNKS
 F32 = jnp.float32
 BF16 = jnp.bfloat16
 MESH = pl.DeviceIdType.MESH
@@ -48,7 +51,7 @@
     bg_hbm,
     lon_hbm,
     lat_ref,
-    out_hbm,
+    out_v,
     w_v,
     masked,
     values,
@@ -58,11 +61,9 @@
     field,
     along,
     lon_v,
-    out_v,
     w_sem,
     bg_sem,
     lon_sem,
-    out_sem,
     box_send,
     box_recv,
     halo_send,
@@ -223,14 +224,15 @@
     def _():
         along[:, pl.ds(REACH + LAT_DEV, REACH), :] = jnp.zeros((SLAB_DEV, REACH, NLON), F32)
 
-    def halo_copy(s, up):
+    def halo_copy(s, h, up):
+        columns = pl.ds(h * PIECE, PIECE)
         source = LAT_DEV if up else REACH
         target = 0 if up else REACH + LAT_DEV
         return pltpu.make_async_remote_copy(
-            src_ref=along.at[s, pl.ds(source, REACH)],
-            dst_ref=along.at[s, pl.ds(target, REACH)],
-            send_sem=halo_send.at[s, int(up)],
-            recv_sem=halo_recv.at[s, int(up)],
+            src_ref=along.at[s, pl.ds(source, REACH), columns],
+            dst_ref=along.at[s, pl.ds(target, REACH), columns],
+            send_sem=halo_send.at[s, h, int(up)],
+            recv_sem=halo_recv.at[s, h, int(up)],
             device_id={"band": band + 1 if up else band - 1, "rd": rd},
             device_id_type=MESH,
         )
@@ -289,26 +291,18 @@
             along[s, pl.ds(REACH, LAT_DEV), pl.ds(at, CHUNK)] = total
             return carry
 
-        lax.fori_loop(0, CHUNKS, lon_filter, 0)
-
-        @pl.when(band < n_band - 1)
-        def _(s=s):
-            halo_copy(s, True).start()
-
-        @pl.when(band > 0)
-        def _(s=s):
-            halo_copy(s, False).start()
-
-    out_copies = []
+        for h in range(PIECES):
+            lax.fori_loop(h * PIECE_CHUNKS, (h + 1) * PIECE_CHUNKS, lon_filter, 0)
+
+            @pl.when(band < n_band - 1)
+            def _(s=s, h=h):
+                halo_copy(s, h, True).start()
+
+            @pl.when(band > 0)
+            def _(s=s, h=h):
+                halo_copy(s, h, False).start()
+
     for s in range(SLAB_DEV):
-
-        @pl.when(band > 0)
-        def _(s=s):
-            halo_copy(s, True).wait_recv()
-
-        @pl.when(band < n_band - 1)
-        def _(s=s):
-            halo_copy(s, False).wait_recv()
 
         def lat_filter(c, carry, s=s):
             columns = pl.ds(pl.multiple_of(c * CHUNK, TILE), CHUNK)
@@ -320,9 +314,17 @@
             )
             return carry
 
-        lax.fori_loop(0, CHUNKS, lat_filter, 0)
-        out_copies.append(pltpu.make_async_copy(out_v.at[s], out_hbm.at[s], out_sem.at[s]))
-        out_copies[-1].start()
+        for h in range(PIECES):
+
+            @pl.when(band > 0)
+            def _(s=s, h=h):
+                halo_copy(s, h, True).wait_recv()
+
+            @pl.when(band < n_band - 1)
+            def _(s=s, h=h):
+                halo_copy(s, h, False).wait_recv()
+
+            lax.fori_loop(h * PIECE_CHUNKS, (h + 1) * PIECE_CHUNKS, lat_filter, 0)
 
     for s in range(SLAB_DEV):
 
@@ -331,16 +333,15 @@
             return carry
 
         lax.fori_loop(1, n_src, sent, 0)
-
-        @pl.when(band < n_band - 1)
-        def _(s=s):
-            halo_copy(s, True).wait_send()
-
-        @pl.when(band > 0)
-        def _(s=s):
-            halo_copy(s, False).wait_send()
-
-        out_copies[s].wait()
+        for h in range(PIECES):
+
+            @pl.when(band < n_band - 1)
+            def _(s=s, h=h):
+                halo_copy(s, h, True).wait_send()
+
+            @pl.when(band > 0)
+            def _(s=s, h=h):
+                halo_copy(s, h, False).wait_send()
 
 
 def on_device(
@@ -355,7 +356,7 @@
     dma = pltpu.SemaphoreType.DMA
     return pl.pallas_call(
         functools.partial(kernel, n_band, n_rd, cap),
-        out_shape=jax.ShapeDtypeStruct(background.shape, F32),
+        out_shape=pltpu.VMEM(background.shape, F32),
         in_specs=[
             vmem,
             vmem,
@@ -366,7 +367,7 @@
             hbm,
             vmem,
         ],
-        out_specs=hbm,
+        out_specs=pl.BlockSpec(memory_space=pltpu.VMEM),
         scratch_shapes=[
             pltpu.VMEM((BLK_DEV, OBS, TILE), BF16),
             pltpu.VMEM((BLK_DEV * 2 * SLAB_DEV, OBS), F32),
@@ -377,15 +378,13 @@
             pltpu.VMEM((SLAB_DEV, LAT_DEV, NLON + 2 * TILE), F32),
             pltpu.VMEM((SLAB_DEV, SPAN, NLON), F32),
             pltpu.VMEM((TAPS, NLON), F32),
-            pltpu.VMEM((SLAB_DEV, LAT_DEV, NLON), F32),
             dma((W_PARTS,)),
             dma((SLAB_DEV,)),
             dma,
-            dma((SLAB_DEV,)),
             dma((SLAB_DEV, n_src)),
             dma((SLAB_DEV, n_src)),
-            dma((SLAB_DEV, 2)),
-            dma((SLAB_DEV, 2)),
+            dma((SLAB_DEV, PIECES, 2)),
+            dma((SLAB_DEV, PIECES, 2)),
         ],
         compiler_params=pltpu.CompilerParams(
             collective_id=0, has_side_effects=True, vmem_limit_bytes=56 << 20

time: 38.7 us -> 34 us (0.88)
  Pallas kernels: 36.4 us -> 32.9 us
  local copies, waits for them, and re-layouts: 2.16 us -> 0.93 us
    pallas_call x1, Pallas kernels: 36.4 us -> 32.9 us  [on_device(): pl.pallas_call(functools.partial(kernel, n_band, n_rd, cap), out_shape=pl...]
    unnamed x1, local copies, waits for them, and re-layouts: 2.16 us -> 0.93 us
where the time goes in v3:
time: 34 us; the launch traced here: 33.8 us
  Pallas kernels  32.9 us (97%)
  local copies, waits for them, and re-layouts  0.93 us (3%)
    pallas_call x1, Pallas kernels, on_device(): pl.pallas_call(functools.partial(kernel, n_band, n_rd, cap), out_shape=pl...  32.9 us
    unnamed x1, local copies, waits for them, and re-layouts  0.93 us

profile of v3, /device:TPU:0, one launch (start us, length us, event | category | flops | bytes accessed | tf_op | source)
XLA Modules:
  0.0 33.8 jit_solution(33582270728500482)
XLA Ops:
  0.0 32.9 %shard_map.82 = f32[2,16,7168]{2,1,0:T(8,128)S(1)} custom-call(bf16[128,4,128]{2,1,0:T(4,128)(2,1)} %dep_ref.1, s32[1,128]{1,0:T(1,128)} %bitcast.3, s32[1,128]{1,0:T(1,128)} %bitcast.4, s32[1,128]{1,0:T(1,128)} %bitcast.5, bf16[128,128,128]{2,1,0:T(8,128)(2,1)} %w_hbm.1, f32[2,16,7168]{2,1,0:T(8,128)} %bg_hbm.1, f32[17,7168]{1,0:T(8,128)} %lon_hbm.1, ...), custom_call_target="tpu_custom_call" | custom-call | tf_op jit(solution)/shard_map/pallas_call | solution.py:357
  32.9 0.9 %copy.10 = f32[2,16,7168]{2,1,0:T(8,128)} copy(f32[2,16,7168]{2,1,0:T(8,128)S(1)} %shard_map.82) | data formatting | bytes 1835008
